TPU v7x, 32 devices: a whole 2x2x4 slice. The times are simulated.
32 devices in a mesh: doc: 8 (over z, x), tensor: 4 (over y, core).
Axes of the slice: x: 2, y: 2, z: 4, core: 2. Of those that a mesh axis runs over, the one named last changes fastest.
Arguments:
- hidden: bfloat16 [2048, 14336], P('doc', 'tensor'), may hold values from -33 to 33
- grads: bfloat16 [2048, 4096], P('doc'), may hold values from -61 to 61
- lengths: int32 [16], P('doc'), may hold values from 64 to 128, as said below
Outputs:
- grad_weight: float32 [4096, 14336], P('doc', 'tensor')
- norm_ratio: float32 [16], P('doc')
Inputs may be any that keep to these rules, and one draw needn't show every extreme that they name: `lengths`: the valid tokens of a document are the first ones of its slot; some document fills its slot.
All inputs are finite; a program needn't handle non-finite values.
Results may differ from a plain program's by a relative error of at most 0.0003.
Values may be sent and summed in bfloat16 or wider, within the bound.
A program may use at most 128 MiB of HBM per device.

v0:
```python
import math

import jax
import jax.numpy as jnp
from jax import lax
from jax.sharding import PartitionSpec as P

D = 4096
FF = 14336
SLOT = 128


clip_ratio = 2.0
epsilon = 1e-06


def weighted_sum(grad_blocks, hidden_blocks, weights):

    def step_fn(running, inputs):
        grad_one, hidden_one, weight_one = inputs
        product = lax.dot_general(
            grad_one, hidden_one, (((0,), (0,)), ((), ())), preferred_element_type=jnp.float32
        )
        return (running + weight_one * product, None)

    start_value = jnp.zeros((grad_blocks.shape[2], hidden_blocks.shape[2]), jnp.float32)
    running, unused = lax.scan(step_fn, start_value, (grad_blocks, hidden_blocks, weights))
    return running


def per_device(hidden, grads, lengths):
    doc_here = lengths.shape[0]
    ff_local = hidden.shape[1]
    model_dim = grads.shape[1]
    hidden_docs = hidden.reshape(doc_here, SLOT, ff_local)
    positions = jnp.arange(SLOT, dtype=jnp.int32)
    in_length = positions[None, :] < lengths[:, None]
    grad_docs = jnp.where(
        in_length[:, :, None], grads.reshape(doc_here, SLOT, model_dim), jnp.zeros((), grads.dtype)
    )
    hidden_gram = jnp.einsum(
        "nsf,ntf->nst", hidden_docs, hidden_docs, preferred_element_type=jnp.float32
    )
    grad_gram = jnp.einsum("nsd,ntd->nst", grad_docs, grad_docs, preferred_element_type=jnp.float32)
    partial_squares = jnp.sum(hidden_gram * grad_gram, axis=(1, 2))
    squares = lax.psum(partial_squares, "tensor")
    doc_total = doc_here * lax.axis_size("doc")
    clip_norm = clip_ratio * math.sqrt(SLOT * FF * D)
    norm_ratio = jnp.sqrt(squares + epsilon) / clip_norm
    weights = jnp.minimum(1.0, 1.0 / norm_ratio) / (clip_ratio * math.sqrt(SLOT * doc_total))
    all_weights = lax.all_gather(weights, "doc", axis=0, tiled=True)
    columns = lax.all_to_all(
        grad_docs.reshape(doc_here * SLOT, model_dim),
        "doc",
        split_axis=1,
        concat_axis=0,
        tiled=True,
    )
    col_width = columns.shape[1]
    shard_rows = lax.all_gather(hidden, "doc", axis=0, tiled=True)
    doc_span = shard_rows.shape[0] // SLOT
    grad_rows = columns.reshape(doc_span, SLOT, col_width)
    hidden_rows = shard_rows.reshape(doc_span, SLOT, ff_local)
    grad_weight = weighted_sum(grad_rows, hidden_rows, all_weights)
    return (grad_weight, norm_ratio)


def solution(mesh):
    in_specs = (P("doc", "tensor"), P("doc", None), P("doc"))
    out_specs = (P("doc", "tensor"), P("doc"))
    return jax.shard_map(
        per_device, mesh=mesh, in_specs=in_specs, out_specs=out_specs, check_vma=False
    )
```

profile of v0, /device:TPU:8, one launch (start us, length us, event | category | flops | bytes accessed | tf_op | source)
XLA Modules:
  0.0 399.2 jit_solution(1362336004820192045)
XLA Ops:
  7.2 0.0 all-gather.2.cloned.1.call-start
  7.2 0.7 all-gather.2.cloned.1.call-update
  7.9 0.7 fusion.11
  8.6 1.8 broadcast_select_fusion
  10.4 1.5 copy.8
  11.9 6.4 %all-to-all-start = ((bf16[256,8,512]{2,0,1:T(8,128)(2,1)}), bf16[256,8,512]{2,0,1:T(8,128)(2,1)}, u32[]{:S(2)}, u32[]{:S(2)}) async-start(bf16[256,8,512]{2,0,1:T(8,128)(2,1)} %bitcast.21), calls=%async_computation | async-start | bytes 4194304 | tf_op jit(solution)/shard_map/all_to_all | solution.py:52
  18.3 0.8 fusion.5
  19.1 0.0 copy-start.2
  19.1 1.0 copy-done
  20.1 0.7 fusion.8
  20.8 6.3 %psum.7 = f32[2]{0:T(128)S(1)} all-reduce(f32[2]{0:T(128)S(1)} %fusion.8), channel_id=1, replica_groups=mesh['doc'=8,'tensor'=4] {'tensor'}, use_global_device_ids=true, to_apply=%region_1.2 | all-reduce | flops 2 | bytes 16 | tf_op jit(solution)/shard_map/psum | solution.py:46
  27.1 0.6 dynamic-slice
  28.4 0.5 multiply_dynamic-update-slice_fusion
  28.9 95.8 %all-reduce = f32[16]{0:T(128)S(1)} all-reduce(f32[16]{0:T(128)S(1)} %get-tuple-element.58), channel_id=1, replica_groups=mesh['doc'=8,'tensor'=4] {'doc'}, use_global_device_ids=true, to_apply=%add | all-reduce | flops 16 | bytes 128
  124.8 127.8 %all-gather.2.cloned.1.call-done = bf16[2048,3584]{1,0:T(8,128)(2,1)} async-done(((bf16[256,3584]{1,0:T(8,128)(2,1)}), bf16[2048,3584]{1,0:T(8,128)(2,1)}) %all-gather.2.cloned.1.call-update) | async-done | bytes 14680080 | tf_op jit(solution)/shard_map/all_gather | solution.py:60
  252.5 139.8 %while.11 = (s32[]{:T(128)}, f32[512,3584]{1,0:T(8,128)}, f32[16]{0:T(128)S(1)}, bf16[16,128,512]{2,1,0:T(8,128)(2,1)}, bf16[16,128,3584]{2,1,0:T(8,128)(2,1)}, /*index=5*/s32[]{:T(128)}, s32[]{:T(128)}) while((s32[]{:T(128)}, f32[512,3584]{1,0:T(8,128)}, f32[16]{0:T(128)S(1)}, bf16[16,128,512]{2,1,0:T(8,128)(2,1)}, ...), condition=%wide.region_3.4_spmd.clone, body=%wide.region_2.3_spmd.clone.sunk | while | flops 475267072 | bytes 15730275 | solution.py:27
  252.5 0.6 dynamic_slice.28
  253.1 6.1 %select_add_fusion.2 = f32[512,3584]{1,0:T(8,128)} fusion(f32[512,3584]{1,0:T(8,128)} %get-tuple-element.101, f32[]{:T(128)} %bitcast.27, pred[]{:T(512)S(6)} %compare.3, bf16[16,128,3584]{2,1,0:T(8,128)(2,1)} %get-tuple-element.111, s32[]{:T(128)} %get-tuple-element.100, bf16[16,128,512]{2,1,0:T(8,128)(2,1)} %get-tuple-element.110), kind=kOutput, calls=%fused_computation.clone.1 | convolution fusion | flops 475267072 | bytes 15730177 | tf_op jit(solution)/shard_map/while/body/eval_jaxpr/dot_general | solution.py:21
  259.2 0.6 dynamic_slice.28
  259.8 8.3 %select_add_fusion.2 = f32[512,3584]{1,0:T(8,128)} fusion(f32[512,3584]{1,0:T(8,128)} %get-tuple-element.101, f32[]{:T(128)} %bitcast.27, pred[]{:T(512)S(6)} %compare.3, bf16[16,128,3584]{2,1,0:T(8,128)(2,1)} %get-tuple-element.111, s32[]{:T(128)} %get-tuple-element.100, bf16[16,128,512]{2,1,0:T(8,128)(2,1)} %get-tuple-element.110), kind=kOutput, calls=%fused_computation.clone.1 | convolution fusion | flops 475267072 | bytes 15730177 | tf_op jit(solution)/shard_map/while/body/eval_jaxpr/dot_general | solution.py:21
  268.1 0.6 dynamic_slice.28
  268.7 8.3 %select_add_fusion.2 = f32[512,3584]{1,0:T(8,128)} fusion(f32[512,3584]{1,0:T(8,128)} %get-tuple-element.101, f32[]{:T(128)} %bitcast.27, pred[]{:T(512)S(6)} %compare.3, bf16[16,128,3584]{2,1,0:T(8,128)(2,1)} %get-tuple-element.111, s32[]{:T(128)} %get-tuple-element.100, bf16[16,128,512]{2,1,0:T(8,128)(2,1)} %get-tuple-element.110), kind=kOutput, calls=%fused_computation.clone.1 | convolution fusion | flops 475267072 | bytes 15730177 | tf_op jit(solution)/shard_map/while/body/eval_jaxpr/dot_general | solution.py:21
  277.0 0.6 dynamic_slice.28
  277.6 8.3 %select_add_fusion.2 = f32[512,3584]{1,0:T(8,128)} fusion(f32[512,3584]{1,0:T(8,128)} %get-tuple-element.101, f32[]{:T(128)} %bitcast.27, pred[]{:T(512)S(6)} %compare.3, bf16[16,128,3584]{2,1,0:T(8,128)(2,1)} %get-tuple-element.111, s32[]{:T(128)} %get-tuple-element.100, bf16[16,128,512]{2,1,0:T(8,128)(2,1)} %get-tuple-element.110), kind=kOutput, calls=%fused_computation.clone.1 | convolution fusion | flops 475267072 | bytes 15730177 | tf_op jit(solution)/shard_map/while/body/eval_jaxpr/dot_general | solution.py:21
  285.9 0.6 dynamic_slice.28
  286.5 8.3 %select_add_fusion.2 = f32[512,3584]{1,0:T(8,128)} fusion(f32[512,3584]{1,0:T(8,128)} %get-tuple-element.101, f32[]{:T(128)} %bitcast.27, pred[]{:T(512)S(6)} %compare.3, bf16[16,128,3584]{2,1,0:T(8,128)(2,1)} %get-tuple-element.111, s32[]{:T(128)} %get-tuple-element.100, bf16[16,128,512]{2,1,0:T(8,128)(2,1)} %get-tuple-element.110), kind=kOutput, calls=%fused_computation.clone.1 | convolution fusion | flops 475267072 | bytes 15730177 | tf_op jit(solution)/shard_map/while/body/eval_jaxpr/dot_general | solution.py:21
  294.7 0.6 dynamic_slice.28
  295.3 8.3 %select_add_fusion.2 = f32[512,3584]{1,0:T(8,128)} fusion(f32[512,3584]{1,0:T(8,128)} %get-tuple-element.101, f32[]{:T(128)} %bitcast.27, pred[]{:T(512)S(6)} %compare.3, bf16[16,128,3584]{2,1,0:T(8,128)(2,1)} %get-tuple-element.111, s32[]{:T(128)} %get-tuple-element.100, bf16[16,128,512]{2,1,0:T(8,128)(2,1)} %get-tuple-element.110), kind=kOutput, calls=%fused_computation.clone.1 | convolution fusion | flops 475267072 | bytes 15730177 | tf_op jit(solution)/shard_map/while/body/eval_jaxpr/dot_general | solution.py:21
  303.6 0.6 dynamic_slice.28
  304.2 8.3 %select_add_fusion.2 = f32[512,3584]{1,0:T(8,128)} fusion(f32[512,3584]{1,0:T(8,128)} %get-tuple-element.101, f32[]{:T(128)} %bitcast.27, pred[]{:T(512)S(6)} %compare.3, bf16[16,128,3584]{2,1,0:T(8,128)(2,1)} %get-tuple-element.111, s32[]{:T(128)} %get-tuple-element.100, bf16[16,128,512]{2,1,0:T(8,128)(2,1)} %get-tuple-element.110), kind=kOutput, calls=%fused_computation.clone.1 | convolution fusion | flops 475267072 | bytes 15730177 | tf_op jit(solution)/shard_map/while/body/eval_jaxpr/dot_general | solution.py:21
  312.5 0.6 dynamic_slice.28
  313.1 8.3 %select_add_fusion.2 = f32[512,3584]{1,0:T(8,128)} fusion(f32[512,3584]{1,0:T(8,128)} %get-tuple-element.101, f32[]{:T(128)} %bitcast.27, pred[]{:T(512)S(6)} %compare.3, bf16[16,128,3584]{2,1,0:T(8,128)(2,1)} %get-tuple-element.111, s32[]{:T(128)} %get-tuple-element.100, bf16[16,128,512]{2,1,0:T(8,128)(2,1)} %get-tuple-element.110), kind=kOutput, calls=%fused_computation.clone.1 | convolution fusion | flops 475267072 | bytes 15730177 | tf_op jit(solution)/shard_map/while/body/eval_jaxpr/dot_general | solution.py:21
  321.4 0.6 dynamic_slice.28
  322.0 8.3 %select_add_fusion.2 = f32[512,3584]{1,0:T(8,128)} fusion(f32[512,3584]{1,0:T(8,128)} %get-tuple-element.101, f32[]{:T(128)} %bitcast.27, pred[]{:T(512)S(6)} %compare.3, bf16[16,128,3584]{2,1,0:T(8,128)(2,1)} %get-tuple-element.111, s32[]{:T(128)} %get-tuple-element.100, bf16[16,128,512]{2,1,0:T(8,128)(2,1)} %get-tuple-element.110), kind=kOutput, calls=%fused_computation.clone.1 | convolution fusion | flops 475267072 | bytes 15730177 | tf_op jit(solution)/shard_map/while/body/eval_jaxpr/dot_general | solution.py:21
  330.2 0.6 dynamic_slice.28
  330.8 8.3 %select_add_fusion.2 = f32[512,3584]{1,0:T(8,128)} fusion(f32[512,3584]{1,0:T(8,128)} %get-tuple-element.101, f32[]{:T(128)} %bitcast.27, pred[]{:T(512)S(6)} %compare.3, bf16[16,128,3584]{2,1,0:T(8,128)(2,1)} %get-tuple-element.111, s32[]{:T(128)} %get-tuple-element.100, bf16[16,128,512]{2,1,0:T(8,128)(2,1)} %get-tuple-element.110), kind=kOutput, calls=%fused_computation.clone.1 | convolution fusion | flops 475267072 | bytes 15730177 | tf_op jit(solution)/shard_map/while/body/eval_jaxpr/dot_general | solution.py:21
  339.1 0.6 dynamic_slice.28
  339.7 8.3 %select_add_fusion.2 = f32[512,3584]{1,0:T(8,128)} fusion(f32[512,3584]{1,0:T(8,128)} %get-tuple-element.101, f32[]{:T(128)} %bitcast.27, pred[]{:T(512)S(6)} %compare.3, bf16[16,128,3584]{2,1,0:T(8,128)(2,1)} %get-tuple-element.111, s32[]{:T(128)} %get-tuple-element.100, bf16[16,128,512]{2,1,0:T(8,128)(2,1)} %get-tuple-element.110), kind=kOutput, calls=%fused_computation.clone.1 | convolution fusion | flops 475267072 | bytes 15730177 | tf_op jit(solution)/shard_map/while/body/eval_jaxpr/dot_general | solution.py:21
  348.0 0.6 dynamic_slice.28
  348.6 8.3 %select_add_fusion.2 = f32[512,3584]{1,0:T(8,128)} fusion(f32[512,3584]{1,0:T(8,128)} %get-tuple-element.101, f32[]{:T(128)} %bitcast.27, pred[]{:T(512)S(6)} %compare.3, bf16[16,128,3584]{2,1,0:T(8,128)(2,1)} %get-tuple-element.111, s32[]{:T(128)} %get-tuple-element.100, bf16[16,128,512]{2,1,0:T(8,128)(2,1)} %get-tuple-element.110), kind=kOutput, calls=%fused_computation.clone.1 | convolution fusion | flops 475267072 | bytes 15730177 | tf_op jit(solution)/shard_map/while/body/eval_jaxpr/dot_general | solution.py:21
  356.9 0.6 dynamic_slice.28
  357.5 8.3 %select_add_fusion.2 = f32[512,3584]{1,0:T(8,128)} fusion(f32[512,3584]{1,0:T(8,128)} %get-tuple-element.101, f32[]{:T(128)} %bitcast.27, pred[]{:T(512)S(6)} %compare.3, bf16[16,128,3584]{2,1,0:T(8,128)(2,1)} %get-tuple-element.111, s32[]{:T(128)} %get-tuple-element.100, bf16[16,128,512]{2,1,0:T(8,128)(2,1)} %get-tuple-element.110), kind=kOutput, calls=%fused_computation.clone.1 | convolution fusion | flops 475267072 | bytes 15730177 | tf_op jit(solution)/shard_map/while/body/eval_jaxpr/dot_general | solution.py:21
  365.7 0.6 dynamic_slice.28
  366.3 8.3 %select_add_fusion.2 = f32[512,3584]{1,0:T(8,128)} fusion(f32[512,3584]{1,0:T(8,128)} %get-tuple-element.101, f32[]{:T(128)} %bitcast.27, pred[]{:T(512)S(6)} %compare.3, bf16[16,128,3584]{2,1,0:T(8,128)(2,1)} %get-tuple-element.111, s32[]{:T(128)} %get-tuple-element.100, bf16[16,128,512]{2,1,0:T(8,128)(2,1)} %get-tuple-element.110), kind=kOutput, calls=%fused_computation.clone.1 | convolution fusion | flops 475267072 | bytes 15730177 | tf_op jit(solution)/shard_map/while/body/eval_jaxpr/dot_general | solution.py:21
  374.6 0.6 dynamic_slice.28
  375.2 8.3 %select_add_fusion.2 = f32[512,3584]{1,0:T(8,128)} fusion(f32[512,3584]{1,0:T(8,128)} %get-tuple-element.101, f32[]{:T(128)} %bitcast.27, pred[]{:T(512)S(6)} %compare.3, bf16[16,128,3584]{2,1,0:T(8,128)(2,1)} %get-tuple-element.111, s32[]{:T(128)} %get-tuple-element.100, bf16[16,128,512]{2,1,0:T(8,128)(2,1)} %get-tuple-element.110), kind=kOutput, calls=%fused_computation.clone.1 | convolution fusion | flops 475267072 | bytes 15730177 | tf_op jit(solution)/shard_map/while/body/eval_jaxpr/dot_general | solution.py:21
  383.5 0.6 dynamic_slice.28
  384.1 8.3 %select_add_fusion.2 = f32[512,3584]{1,0:T(8,128)} fusion(f32[512,3584]{1,0:T(8,128)} %get-tuple-element.101, f32[]{:T(128)} %bitcast.27, pred[]{:T(512)S(6)} %compare.3, bf16[16,128,3584]{2,1,0:T(8,128)(2,1)} %get-tuple-element.111, s32[]{:T(128)} %get-tuple-element.100, bf16[16,128,512]{2,1,0:T(8,128)(2,1)} %get-tuple-element.110), kind=kOutput, calls=%fused_computation.clone.1 | convolution fusion | flops 475267072 | bytes 15730177 | tf_op jit(solution)/shard_map/while/body/eval_jaxpr/dot_general | solution.py:21
  (7 shorter events, 0.0 us)
Async XLA Ops:
  7.2 245.4 %all-gather.2.cloned.1.call-start = ((), (), s32[]{:S(2)}) async-start(), calls=%async_computation.1 | async-start | bytes 16515072 | tf_op jit(solution)/shard_map/all_gather | solution.py:60
  11.9 6.4 %copy-start.1 = (bf16[256,4096]{1,0:T(8,128)(2,1)S(1)}, bf16[256,4096]{1,0:T(8,128)(2,1)}, u32[]{:S(2)}) copy-start(bf16[256,4096]{1,0:T(8,128)(2,1)} %param.6) | copy-start | bytes 6291460
  11.9 112.8 %all-to-all-start = ((bf16[256,8,512]{2,0,1:T(8,128)(2,1)}), bf16[256,8,512]{2,0,1:T(8,128)(2,1)}, u32[]{:S(2)}, u32[]{:S(2)}) async-start(bf16[256,8,512]{2,0,1:T(8,128)(2,1)} %bitcast.21), calls=%async_computation | async-start | bytes 4194304 | tf_op jit(solution)/shard_map/all_to_all | solution.py:52
  18.3 1.8 copy-start
  19.1 8.0 %copy-start.2 = (u32[32]{0:T(128)S(1)}, u32[32]{0:T(128)}, u32[]{:S(2)}) copy-start(u32[32]{0:T(128)} %constant.29) | copy-start | bytes 388
Sparse Core Ops, SparseCore 0:
  10.2 242.3 all-gather.1
where the time goes:
time: 403 us; the launch traced here: 399 us
  matrix products  132 us (33%)
  waiting for transfers between devices  128 us (32%)
  blocking collectives  102 us (25%)
  between operations  14.7 us (4%)
  local copies, waits for them, and re-layouts  12.8 us (3%)
  starting transfers between devices  6.42 us (2%)
    dot_general x16, matrix products, step_fn(): lax.dot_general(grad_one, hidden_one, (((0,), (0,)), ((), ())), preferred...  130 us
    all_gather x1, waiting for transfers between devices, per_device(): shard_rows = lax.all_gather(hidden, 'doc', axis=0, tiled=True)  128 us
    unnamed x1, blocking collectives  95.8 us
    dynamic_slice x16, local copies, waits for them, and re-layouts, weighted_sum(): lax.scan(step_fn, start_value, (grad_blocks, hidden_blocks, weights))  9.74 us
  transfers between devices with their start and end apart: 2, of which 1 were waited for; matrix products, arithmetic and copies ran while one was open for 2% of the time, Pallas kernels for 0%

commit v1 on v0

v1 whole, which is shorter than its diff:
```python
import functools
import math

import jax
import jax.numpy as jnp
from jax import lax
from jax.experimental import pallas as pl
from jax.experimental.pallas import tpu as pltpu
from jax.sharding import PartitionSpec as P

D = 4096
FF = 14336
SLOT = 128

clip_ratio = 2.0
epsilon = 1e-06
MESH = pl.DeviceIdType.MESH


def kernel(cfg, len_ref, hid, grads, out, nr_ref, G, gv, mrx, mT, acc, sq, wts,
           lsem, gsem, osem, ssem, rsem, ms_s, ms_r, m2_s, m2_r, sq_s, sq_r, w_s, w_r):
    nz, nx, T, C, docs, n_docs = cfg
    n = nz * nx
    me = lax.axis_index("doc")
    t = lax.axis_index("tensor")
    z, x = me // nx, lax.rem(me, nx)
    W = G.shape[3]
    R = G.shape[2]
    Dl = acc.shape[1]
    q = R // T
    trow = pl.ds(pl.multiple_of(t * q, q), q)

    for c in range(C):
        pltpu.make_async_copy(hid.at[:, pl.ds(c * W, W)], G.at[c, me], lsem.at[c]).start()
    pltpu.make_async_copy(grads, gv, gsem).start()

    bar = pltpu.get_barrier_semaphore()
    for k in range(1, n):
        pl.semaphore_signal(bar, inc=1, device_id={"doc": lax.rem(me + k, n), "tensor": t},
                            device_id_type=MESH)
    for k in range(1, T):
        pl.semaphore_signal(bar, inc=1, device_id={"doc": me, "tensor": lax.rem(t + k, T)},
                            device_id_type=MESH)
    pl.semaphore_wait(bar, n - 1 + T - 1)

    def block(s, c, k, to):
        return pltpu.make_async_remote_copy(
            src_ref=G.at[c, s], dst_ref=G.at[c, s], send_sem=ssem.at[s, c, k],
            recv_sem=rsem.at[s, c], device_id={"doc": to, "tensor": t}, device_id_type=MESH)

    up = jnp.minimum(me + nx, n - nx + x)
    down = jnp.maximum(me - nx, x)

    def send_up(s, c):
        @pl.when(z < nz - 1)
        def _():
            block(s, c, 0, up).start()

    def send_down(s, c):
        @pl.when(z > 0)
        def _():
            block(s, c, 1, down).start()

    def send_x(s, c):
        for k in range(1, nx):
            block(s, c, 1 + k, z * nx + lax.rem(x + k, nx)).start()

    def arrive(s, c):
        block(s, c, 0, up).wait_recv()

    for c in range(C):
        pltpu.make_async_copy(hid.at[:, pl.ds(c * W, W)], G.at[c, me], lsem.at[c]).wait()
        send_x(me, c)
        send_up(me, c)
        send_down(me, c)

    pltpu.make_async_copy(grads, gv, gsem).wait()
    for d in range(docs):
        keep = lax.broadcasted_iota(jnp.int32, (SLOT, 512), 0) < len_ref[d]

        @pl.loop(0, gv.shape[1] // 512)
        def _(i):
            cols = pl.ds(pl.multiple_of(i * 512, 512), 512)
            v = gv[d * SLOT:(d + 1) * SLOT, cols]
            gv[d * SLOT:(d + 1) * SLOT, cols] = jnp.where(
                keep, v.astype(jnp.float32), 0.0).astype(v.dtype)

    def share(j, s):
        return pltpu.make_async_remote_copy(
            src_ref=gv.at[trow, pl.ds(pl.multiple_of(j * Dl, Dl), Dl)],
            dst_ref=mrx.at[s, trow, :], send_sem=ms_s.at[j], recv_sem=ms_r.at[s],
            device_id={"doc": j, "tensor": t}, device_id_type=MESH)

    for k in range(1, n):
        share(lax.rem(me + k, n), me).start()

    def nt(a, b):
        return lax.dot_general(a, b, (((1,), (1,)), ((), ())),
                               preferred_element_type=jnp.float32)

    row = lax.broadcasted_iota(jnp.int32, (8, 128), 0)
    part = jnp.zeros((8, 128), jnp.float32)
    zero = jnp.zeros((SLOT, SLOT), jnp.float32)
    for d in range(docs):
        rows = slice(d * SLOT, (d + 1) * SLOT)

        def hid_step(c, run):
            h = G[c, me, rows, :]
            return run + nt(h, h)

        def grad_step(i, run):
            m = gv[rows, pl.ds(pl.multiple_of(i * 512, 512), 512)]
            return run + nt(m, m)

        hg = lax.fori_loop(0, C, hid_step, zero)
        gg = lax.fori_loop(0, gv.shape[1] // 512, grad_step, zero)
        one = jnp.sum(jnp.sum(hg * gg, axis=1, keepdims=True), axis=0, keepdims=True)
        part = jnp.where(row == d, one, part)
    sq[t] = part

    def sq_copy(tt, src):
        return pltpu.make_async_remote_copy(
            src_ref=sq.at[src], dst_ref=sq.at[src], send_sem=sq_s.at[tt],
            recv_sem=sq_r.at[src], device_id={"doc": me, "tensor": tt}, device_id_type=MESH)

    for k in range(1, T):
        sq_copy(lax.rem(t + k, T), t).start()
    mT[me] = gv[:, pl.ds(pl.multiple_of(me * Dl, Dl), Dl)].T
    for k in range(1, T):
        o = lax.rem(t + k, T)
        sq_copy(o, o).wait_recv()
    total = sq[0]
    for k in range(1, T):
        total = total + sq[k]
    clip_norm = clip_ratio * math.sqrt(SLOT * FF * D)
    ratio = jnp.sqrt(total + epsilon) / clip_norm
    nr_ref[...] = ratio
    wts[me] = jnp.minimum(1.0, 1.0 / ratio) / (clip_ratio * math.sqrt(SLOT * n_docs))

    def w_copy(j, s):
        return pltpu.make_async_remote_copy(
            src_ref=wts.at[s], dst_ref=wts.at[s], send_sem=w_s.at[j], recv_sem=w_r.at[s],
            device_id={"doc": j, "tensor": t}, device_id_type=MESH)

    for k in range(1, n):
        w_copy(lax.rem(me + k, n), me).start()

    def spread(s, tt, o):
        rr = pl.ds(pl.multiple_of(o * q, q), q)
        return pltpu.make_async_remote_copy(
            src_ref=mrx.at[s, rr, :], dst_ref=mrx.at[s, rr, :], send_sem=m2_s.at[s, tt],
            recv_sem=m2_r.at[s, o], device_id={"doc": me, "tensor": tt}, device_id_type=MESH)

    @pl.loop(1, n)
    def _(k):
        s = lax.rem(me + k, n)
        share(s, s).wait_recv()
        for kk in range(1, T):
            spread(s, lax.rem(t + kk, T), t).start()

    def product(s, c, first):
        tile = min(256, Dl)
        for r in range(Dl // tile):
            rr = slice(r * tile, (r + 1) * tile)
            tot = None
            for d in range(docs):
                p = jnp.dot(mT[s, rr, d * SLOT:(d + 1) * SLOT],
                            G[c, s, d * SLOT:(d + 1) * SLOT, :],
                            preferred_element_type=jnp.float32)
                p = p * wts[s, d:d + 1, 0:1]
                tot = p if tot is None else tot + p
            acc[c, rr, :] = tot if first else acc[c, rr, :] + tot

    @pl.loop(0, C)
    def _(c):
        product(me, c, True)

    for k in range(1, nx):
        s = z * nx + lax.rem(x + k, nx)
        arrive(s, 0)
        send_up(s, 0)
        send_down(s, 0)

    @pl.loop(1, n)
    def _(k):
        s = lax.rem(me + k, n)
        for kk in range(1, T):
            o = lax.rem(t + kk, T)
            spread(s, o, o).wait_recv()
        w_copy(s, s).wait_recv()
        mT[s] = mrx[s].T

    def out_copy(c):
        return pltpu.make_async_copy(acc.at[c], out.at[:, pl.ds(pl.multiple_of(c * W, W), W)],
                                     osem.at[c])

    for dist in range(1, nz + 1):
        def step(c, dist=dist):
            if dist < nz:
                for sign, send in ((-1, send_up), (1, send_down)):
                    sz = z + sign * dist

                    @pl.when((sz >= 0) & (sz < nz))
                    def _():
                        s = sz * nx + x
                        arrive(s, c)
                        send(s, c)

                        @pl.when(c > 0)
                        def _():
                            send_x(s, c)

                        @pl.when(c == 0)
                        def _():
                            for k in range(1, nx):
                                s2 = sz * nx + lax.rem(x + k, nx)
                                arrive(s2, 0)
                                send(s2, 0)
                                product(s2, 0, False)

                        product(s, c, False)
            for sign in ((-1, 1) if dist > 1 else (1,)):
                sz = z + sign * (dist - 1)

                @pl.when((sz >= 0) & (sz < nz))
                def _():
                    for k in range(1, nx):
                        s = sz * nx + lax.rem(x + k, nx)
                        if dist == 1:
                            @pl.when(c > 0)
                            def _():
                                arrive(s, c)
                            product(s, c, False)
                        else:
                            @pl.when(c > 0)
                            def _():
                                arrive(s, c)
                                product(s, c, False)
            if dist == nz:
                out_copy(c).start()

        pl.loop(0, C)(step)

    for k in range(1, T):
        sq_copy(lax.rem(t + k, T), t).wait_send()

    @pl.loop(1, n)
    def _(k):
        j = lax.rem(me + k, n)
        share(j, me).wait_send()
        w_copy(j, me).wait_send()
        for kk in range(1, T):
            spread(j, lax.rem(t + kk, T), t).wait_send()

    @pl.loop(0, n)
    def _(s):
        sz, sx = s // nx, lax.rem(s, nx)

        @pl.loop(0, C)
        def _(c):
            along = (sx == x) | (c == 0)

            @pl.when(along & (z < nz - 1) & (sz <= z))
            def _():
                block(s, c, 0, up).wait_send()

            @pl.when(along & (z > 0) & (sz >= z))
            def _():
                block(s, c, 1, down).wait_send()

            @pl.when((sx == x) & ((c > 0) | (sz == z)))
            def _():
                for k in range(1, nx):
                    block(s, c, 1 + k, z * nx + lax.rem(x + k, nx)).wait_send()

    @pl.loop(0, C)
    def _(c):
        out_copy(c).wait()


def per_device(hidden, grads, lengths, *, n, T):
    docs = lengths.shape[0]
    R, ffl = hidden.shape
    dm = grads.shape[1]
    Dl = dm // n
    nx = max(k for k in range(1, n + 1) if n % k == 0 and k * k <= n)
    nz = n // nx
    C = next(k for k in (7, 8, 4, 2, 1) if ffl % (128 * k) == 0)
    W = ffl // C
    dma = pltpu.SemaphoreType.DMA
    f32, bf16 = jnp.float32, hidden.dtype
    gw, nr = pl.pallas_call(
        functools.partial(kernel, (nz, nx, T, C, docs, docs * n)),
        out_shape=(jax.ShapeDtypeStruct((Dl, ffl), f32), jax.ShapeDtypeStruct((8, 128), f32)),
        in_specs=[pl.BlockSpec(memory_space=pltpu.SMEM), pl.BlockSpec(memory_space=pl.ANY),
                  pl.BlockSpec(memory_space=pl.ANY)],
        out_specs=(pl.BlockSpec(memory_space=pl.ANY), pl.BlockSpec(memory_space=pltpu.VMEM)),
        scratch_shapes=[
            pltpu.VMEM((C, n, R, W), bf16),
            pltpu.VMEM((R, dm), bf16),
            pltpu.VMEM((n, R, Dl), bf16),
            pltpu.VMEM((n, Dl, R), bf16),
            pltpu.VMEM((C, Dl, W), f32),
            pltpu.VMEM((T, 8, 128), f32),
            pltpu.VMEM((n, 8, 128), f32),
            dma((C,)), dma, dma((C,)),
            dma((n, C, 1 + nx)), dma((n, C)),
            dma((n,)), dma((n,)), dma((n, T)), dma((n, T)),
            dma((T,)), dma((T,)), dma((n,)), dma((n,)),
        ],
        compiler_params=pltpu.CompilerParams(
            collective_id=0, has_side_effects=True, vmem_limit_bytes=56 * 2**20),
        cost_estimate=pl.CostEstimate(flops=2 * R * n * Dl * ffl, transcendentals=0,
                                      bytes_accessed=4 * Dl * ffl + 2 * R * (ffl + dm)),
    )(lengths, hidden, grads)
    return gw, nr[:docs, 0]


def solution(mesh):
    in_specs = (P("doc", "tensor"), P("doc", None), P("doc"))
    out_specs = (P("doc", "tensor"), P("doc"))
    body = functools.partial(per_device, n=mesh.shape["doc"], T=mesh.shape["tensor"])
    return jax.shard_map(
        body, mesh=mesh, in_specs=in_specs, out_specs=out_specs, check_vma=False
    )
```

time: 403 us -> 199 us (0.49)
  Pallas kernels: 0 us -> 190 us
  matrix products: 132 us -> 0 us
  waiting for transfers between devices: 128 us -> 0 us
  blocking collectives: 102 us -> 0 us
  between operations: 14.7 us -> 0.64 us
  starting transfers between devices: 6.42 us -> 0 us
  local copies, waits for them, and re-layouts: 12.8 us -> 7.91 us
    pallas_call x0 -> x1, Pallas kernels: none -> 190 us  [per_device(): pl.pallas_call(functools.partial(kernel, (nz, nx, T, C, docs, docs * n)),...]
    dot_general x18 -> x0, matrix products: 132 us -> none  [the longest x16 130 us: step_fn(): lax.dot_general(grad_one, hidden_one, (((0,), (0,)), ((), ())), preferred...]
    all_gather x1 -> x0, waiting for transfers between devices: 128 us -> none  [per_device(): shard_rows = lax.all_gather(hidden, 'doc', axis=0, tiled=True)]
    unnamed x1 -> x0, blocking collectives: 95.8 us -> none
    dynamic_slice x16 -> x0, local copies, waits for them, and re-layouts: 9.74 us -> none  [weighted_sum(): lax.scan(step_fn, start_value, (grad_blocks, hidden_blocks, weights))]
    all_to_all x1 -> x0, starting transfers between devices: 6.38 us -> none  [per_device(): lax.all_to_all(grad_docs.reshape(doc_here * SLOT, model_dim), 'doc', spli...]
    psum x1 -> x0, blocking collectives: 6.28 us -> none  [per_device(): squares = lax.psum(partial_squares, 'tensor')]
    unnamed x8 -> x1, local copies, waits for them, and re-layouts: 1.56 us -> 6.6 us
  transfers between devices with their start and end apart: 2 -> 0, of which waited for: 1 -> 0; matrix products, arithmetic and copies ran while one was open for 2% -> 0% of each run, Pallas kernels for 0% -> 0%
where the time goes in v1:
time: 199 us; the launch traced here: 198 us
  Pallas kernels  190 us (95%)
  local copies, waits for them, and re-layouts  7.91 us (4%)
    pallas_call x1, Pallas kernels, per_device(): pl.pallas_call(functools.partial(kernel, (nz, nx, T, C, docs, docs * n)),...  190 us
    unnamed x1, local copies, waits for them, and re-layouts  6.6 us

profile of v1, /device:TPU:8, one launch (start us, length us, event | category | flops | bytes accessed | tf_op | source)
XLA Modules:
  0.0 198.3 jit_solution(3711216268032367395)
XLA Ops:
  0.6 189.8 %shard_map.50 = (f32[512,3584]{1,0:T(8,128)}, f32[8,128]{1,0:T(8,128)}) custom-call(s32[2]{0:T(128)} %len_ref.1, bf16[256,3584]{1,0:T(8,128)(2,1)} %hid.1, bf16[256,4096]{1,0:T(8,128)(2,1)} %grads.1), custom_call_target="tpu_custom_call" | custom-call | flops 7516192768 | bytes 11272192 | tf_op jit(solution)/shard_map/pallas_call | solution.py:292
  190.4 1.3 slice_reduce_fusion
  191.7 6.6 %copy.6 = f32[512,3584]{1,0:T(8,128)} copy(f32[512,3584]{1,0:T(8,128)} %get-tuple-element.8) | data formatting | bytes 14680064

commit v2 on v1

--- a/solution.py
+++ b/solution.py
@@ -19,7 +19,7 @@
 
 def kernel(cfg, len_ref, hid, grads, out, nr_ref, G, gv, mrx, mT, acc, sq, wts,
            lsem, gsem, osem, ssem, rsem, ms_s, ms_r, m2_s, m2_r, sq_s, sq_r, w_s, w_r):
-    nz, nx, T, C, docs, n_docs = cfg
+    nz, nx, T, C, dup, docs, n_docs = cfg
     n = nz * nx
     me = lax.axis_index("doc")
     t = lax.axis_index("tensor")
@@ -28,6 +28,7 @@
     R = G.shape[2]
     Dl = acc.shape[1]
     q = R // T
+    early = min(3, C)
     trow = pl.ds(pl.multiple_of(t * q, q), q)
 
     for c in range(C):
@@ -68,11 +69,17 @@
     def arrive(s, c):
         block(s, c, 0, up).wait_recv()
 
-    for c in range(C):
+    def land(c):
         pltpu.make_async_copy(hid.at[:, pl.ds(c * W, W)], G.at[c, me], lsem.at[c]).wait()
+
+    def send_own(c):
         send_x(me, c)
         send_up(me, c)
         send_down(me, c)
+
+    for c in range(early):
+        land(c)
+        send_own(c)
 
     pltpu.make_async_copy(grads, gv, gsem).wait()
     for d in range(docs):
@@ -98,6 +105,8 @@
         return lax.dot_general(a, b, (((1,), (1,)), ((), ())),
                                preferred_element_type=jnp.float32)
 
+    for c in range(early, C):
+        land(c)
     row = lax.broadcasted_iota(jnp.int32, (8, 128), 0)
     part = jnp.zeros((8, 128), jnp.float32)
     zero = jnp.zeros((SLOT, SLOT), jnp.float32)
@@ -144,19 +153,14 @@
 
     for k in range(1, n):
         w_copy(lax.rem(me + k, n), me).start()
+    for c in range(early, C):
+        send_own(c)
 
     def spread(s, tt, o):
         rr = pl.ds(pl.multiple_of(o * q, q), q)
         return pltpu.make_async_remote_copy(
             src_ref=mrx.at[s, rr, :], dst_ref=mrx.at[s, rr, :], send_sem=m2_s.at[s, tt],
             recv_sem=m2_r.at[s, o], device_id={"doc": me, "tensor": tt}, device_id_type=MESH)
-
-    @pl.loop(1, n)
-    def _(k):
-        s = lax.rem(me + k, n)
-        share(s, s).wait_recv()
-        for kk in range(1, T):
-            spread(s, lax.rem(t + kk, T), t).start()
 
     def product(s, c, first):
         tile = min(256, Dl)
@@ -171,15 +175,79 @@
                 tot = p if tot is None else tot + p
             acc[c, rr, :] = tot if first else acc[c, rr, :] + tot
 
+    for k in range(1, nx):
+        s = z * nx + lax.rem(x + k, nx)
+        for c in range(dup):
+            arrive(s, c)
+            send_up(s, c)
+            send_down(s, c)
+
+    def out_copy(c):
+        return pltpu.make_async_copy(acc.at[c], out.at[:, pl.ds(pl.multiple_of(c * W, W), W)],
+                                     osem.at[c])
+
+    def each_side(dist, fn):
+        for sign, send in ((-1, send_up), (1, send_down)):
+            sz = z + sign * dist
+
+            @pl.when((sz >= 0) & (sz < nz))
+            def _():
+                fn(sz, send)
+
+    def forward(dist, c):
+        def one(sz, send):
+            s = sz * nx + x
+            arrive(s, c)
+            send(s, c)
+
+            @pl.when(c >= dup)
+            def _():
+                send_x(s, c)
+
+            @pl.when(c < dup)
+            def _():
+                for k in range(1, nx):
+                    s2 = sz * nx + lax.rem(x + k, nx)
+                    arrive(s2, c)
+                    send(s2, c)
+
+        each_side(dist, one)
+
+    def multiply(dist, c):
+        def one(sz, send):
+            product(sz * nx + x, c, False)
+            for k in range(1, nx):
+                s = sz * nx + lax.rem(x + k, nx)
+
+                @pl.when(c >= dup)
+                def _():
+                    arrive(s, c)
+
+                product(s, c, False)
+
+        if dist:
+            each_side(dist, one)
+        else:
+            product(me, c, True)
+            for k in range(1, nx):
+                s = z * nx + lax.rem(x + k, nx)
+
+                @pl.when(c >= dup)
+                def _():
+                    arrive(s, c)
+
+                product(s, c, False)
+
     @pl.loop(0, C)
     def _(c):
-        product(me, c, True)
-
-    for k in range(1, nx):
-        s = z * nx + lax.rem(x + k, nx)
-        arrive(s, 0)
-        send_up(s, 0)
-        send_down(s, 0)
+        forward(1, c)
+
+    @pl.loop(1, n)
+    def _(k):
+        s = lax.rem(me + k, n)
+        share(s, s).wait_recv()
+        for kk in range(1, T):
+            spread(s, lax.rem(t + kk, T), t).start()
 
     @pl.loop(1, n)
     def _(k):
@@ -190,52 +258,13 @@
         w_copy(s, s).wait_recv()
         mT[s] = mrx[s].T
 
-    def out_copy(c):
-        return pltpu.make_async_copy(acc.at[c], out.at[:, pl.ds(pl.multiple_of(c * W, W), W)],
-                                     osem.at[c])
-
-    for dist in range(1, nz + 1):
+    for dist in range(2, nz + 1):
         def step(c, dist=dist):
             if dist < nz:
-                for sign, send in ((-1, send_up), (1, send_down)):
-                    sz = z + sign * dist
-
-                    @pl.when((sz >= 0) & (sz < nz))
-                    def _():
-                        s = sz * nx + x
-                        arrive(s, c)
-                        send(s, c)
-
-                        @pl.when(c > 0)
-                        def _():
-                            send_x(s, c)
-
-                        @pl.when(c == 0)
-                        def _():
-                            for k in range(1, nx):
-                                s2 = sz * nx + lax.rem(x + k, nx)
-                                arrive(s2, 0)
-                                send(s2, 0)
-                                product(s2, 0, False)
-
-                        product(s, c, False)
-            for sign in ((-1, 1) if dist > 1 else (1,)):
-                sz = z + sign * (dist - 1)
-
-                @pl.when((sz >= 0) & (sz < nz))
-                def _():
-                    for k in range(1, nx):
-                        s = sz * nx + lax.rem(x + k, nx)
-                        if dist == 1:
-                            @pl.when(c > 0)
-                            def _():
-                                arrive(s, c)
-                            product(s, c, False)
-                        else:
-                            @pl.when(c > 0)
-                            def _():
-                                arrive(s, c)
-                                product(s, c, False)
+                forward(dist, c)
+            if dist == 2:
+                multiply(0, c)
+            multiply(dist - 1, c)
             if dist == nz:
                 out_copy(c).start()
 
@@ -258,7 +287,7 @@
 
         @pl.loop(0, C)
         def _(c):
-            along = (sx == x) | (c == 0)
+            along = (sx == x) | (c < dup)
 
             @pl.when(along & (z < nz - 1) & (sz <= z))
             def _():
@@ -268,7 +297,7 @@
             def _():
                 block(s, c, 1, down).wait_send()
 
-            @pl.when((sx == x) & ((c > 0) | (sz == z)))
+            @pl.when((sx == x) & ((c >= dup) | (sz == z)))
             def _():
                 for k in range(1, nx):
                     block(s, c, 1 + k, z * nx + lax.rem(x + k, nx)).wait_send()
@@ -286,11 +315,12 @@
     nx = max(k for k in range(1, n + 1) if n % k == 0 and k * k <= n)
     nz = n // nx
     C = next(k for k in (7, 8, 4, 2, 1) if ffl % (128 * k) == 0)
+    dup = C // 7
     W = ffl // C
     dma = pltpu.SemaphoreType.DMA
     f32, bf16 = jnp.float32, hidden.dtype
     gw, nr = pl.pallas_call(
-        functools.partial(kernel, (nz, nx, T, C, docs, docs * n)),
+        functools.partial(kernel, (nz, nx, T, C, dup, docs, docs * n)),
         out_shape=(jax.ShapeDtypeStruct((Dl, ffl), f32), jax.ShapeDtypeStruct((8, 128), f32)),
         in_specs=[pl.BlockSpec(memory_space=pltpu.SMEM), pl.BlockSpec(memory_space=pl.ANY),
                   pl.BlockSpec(memory_space=pl.ANY)],
@@ -309,7 +339,7 @@
             dma((T,)), dma((T,)), dma((n,)), dma((n,)),
         ],
         compiler_params=pltpu.CompilerParams(
-            collective_id=0, has_side_effects=True, vmem_limit_bytes=56 * 2**20),
+            collective_id=0, has_side_effects=True, vmem_limit_bytes=40 * 2**20),
         cost_estimate=pl.CostEstimate(flops=2 * R * n * Dl * ffl, transcendentals=0,
                                       bytes_accessed=4 * Dl * ffl + 2 * R * (ffl + dm)),
     )(lengths, hidden, grads)

time: 199 us -> 179 us (0.90)
  Pallas kernels: 190 us -> 171 us
    pallas_call x1, Pallas kernels: 190 us -> 171 us  [per_device(): pl.pallas_call(functools.partial(kernel, (nz, nx, T, C, dup, docs, docs *...]
    unnamed x1 -> x7, local copies, waits for them, and re-layouts: 6.6 us -> 6.79 us
where the time goes in v2:
time: 179 us
  Pallas kernels  171 us (96%)
  local copies, waits for them, and re-layouts  7.41 us (4%)
    pallas_call x1, Pallas kernels, per_device(): pl.pallas_call(functools.partial(kernel, (nz, nx, T, C, dup, docs, docs *...  171 us
    unnamed x7, local copies, waits for them, and re-layouts  6.79 us

profile of v2, /device:TPU:8, one launch (start us, length us, event | category | flops | bytes accessed | tf_op | source)
XLA Modules:
  0.0 178.9 jit_solution(7337606438270926599)
XLA Ops:
  0.6 0.0 copy-start
  0.6 1.6 copy-done
  2.2 0.0 copy-start.1
  2.2 1.5 copy-done.1
  3.7 0.0 copy-start.2
  3.7 0.7 copy-done.2
  4.4 170.9 %shard_map.50 = (f32[512,3584]{1,0:T(8,128)S(1)}, f32[8,128]{1,0:T(8,128)S(1)}) custom-call(s32[2]{0:T(128)S(1)} %copy-done.2, bf16[256,3584]{1,0:T(8,128)(2,1)S(1)} %copy-done.1, bf16[256,4096]{1,0:T(8,128)(2,1)S(1)} %copy-done), custom_call_target="tpu_custom_call" | custom-call | flops 7516192768 | bytes 11272192 | tf_op jit(solution)/shard_map/pallas_call | solution.py:322
  175.2 0.6 slice_reduce_fusion
  175.9 3.0 %copy.6 = f32[512,3584]{1,0:T(8,128)} copy(f32[512,3584]{1,0:T(8,128)S(1)} %get-tuple-element.8) | data formatting | bytes 14680064
Async XLA Ops:
  0.6 1.6 copy-start
  2.2 1.5 copy-start.1
  3.7 0.7 copy-start.2

commit v3 on v2

--- a/solution.py
+++ b/solution.py
@@ -322,8 +322,8 @@
     gw, nr = pl.pallas_call(
         functools.partial(kernel, (nz, nx, T, C, dup, docs, docs * n)),
         out_shape=(jax.ShapeDtypeStruct((Dl, ffl), f32), jax.ShapeDtypeStruct((8, 128), f32)),
-        in_specs=[pl.BlockSpec(memory_space=pltpu.SMEM), pl.BlockSpec(memory_space=pl.ANY),
-                  pl.BlockSpec(memory_space=pl.ANY)],
+        in_specs=[pl.BlockSpec(memory_space=pltpu.SMEM), pl.BlockSpec(memory_space=pltpu.HBM),
+                  pl.BlockSpec(memory_space=pltpu.HBM)],
         out_specs=(pl.BlockSpec(memory_space=pl.ANY), pl.BlockSpec(memory_space=pltpu.VMEM)),
         scratch_shapes=[
             pltpu.VMEM((C, n, R, W), bf16),
@@ -342,7 +342,7 @@
             collective_id=0, has_side_effects=True, vmem_limit_bytes=40 * 2**20),
         cost_estimate=pl.CostEstimate(flops=2 * R * n * Dl * ffl, transcendentals=0,
                                       bytes_accessed=4 * Dl * ffl + 2 * R * (ffl + dm)),
-    )(lengths, hidden, grads)
+    )(lengths, pltpu.with_memory_space_constraint(hidden, pltpu.HBM), pltpu.with_memory_space_constraint(grads, pltpu.HBM))
     return gw, nr[:docs, 0]
 
 

time: 179 us -> 176 us (0.983)
  local copies, waits for them, and re-layouts: 7.41 us -> 4.32 us
    unnamed x7 -> x3, local copies, waits for them, and re-layouts: 6.79 us -> 3.7 us
where the time goes in v3:
time: 176 us
  Pallas kernels  171 us (97%)
  local copies, waits for them, and re-layouts  4.32 us (2%)
    pallas_call x1, Pallas kernels, per_device(): pl.pallas_call(functools.partial(kernel, (nz, nx, T, C, dup, docs, docs *...  171 us
    unnamed x3, local copies, waits for them, and re-layouts  3.7 us

profile of v3, /device:TPU:8, one launch (start us, length us, event | category | flops | bytes accessed | tf_op | source)
XLA Modules:
  0.0 175.6 jit_solution(16283845027745071442)
XLA Ops:
  0.6 0.0 copy-start
  0.6 0.6 copy-done
  1.3 170.6 %shard_map.50 = (f32[512,3584]{1,0:T(8,128)S(1)}, f32[8,128]{1,0:T(8,128)S(1)}) custom-call(s32[2]{0:T(128)S(1)} %copy-done, bf16[256,3584]{1,0:T(8,128)(2,1)} %hid.1, bf16[256,4096]{1,0:T(8,128)(2,1)} %grads.1), custom_call_target="tpu_custom_call" | custom-call | flops 7516192768 | bytes 11272192 | tf_op jit(solution)/shard_map/pallas_call | solution.py:322
  171.9 0.6 slice_reduce_fusion
  172.5 3.0 %copy.6 = f32[512,3584]{1,0:T(8,128)} copy(f32[512,3584]{1,0:T(8,128)S(1)} %get-tuple-element.8) | data formatting | bytes 14680064
Async XLA Ops:
  0.6 0.7 copy-start
